TPU v7x, 32 devices: a whole 2x2x4 slice. The times are simulated.
32 devices in a mesh: fsdp: 4 (over y, core), ctx: 4 (over z), tp: 2 (over x).
Axes of the slice: x: 2, y: 2, z: 4, core: 2. Of those that a mesh axis runs over, the one named last changes fastest.
Arguments:
- tokens: bfloat16 [8, 2048, 960], P('fsdp', ('ctx', 'tp')), may hold values from -6 to 6
- cotangent: bfloat16 [8, 2048, 960], P('fsdp', ('ctx', 'tp')), may hold values from -6 to 6
- input_gain: bfloat16 [960], P('fsdp'), may hold values from 0.099609375 to 1.8984375
- w_query: bfloat16 [960, 960], P('fsdp'), may hold values from -0.1875 to 0.1875
- w_keyval: bfloat16 [960, 640], P('fsdp'), may hold values from -0.1875 to 0.1875
- w_output: bfloat16 [960, 960], P('fsdp'), may hold values from -2 to 2
- middle_gain: bfloat16 [960], P('fsdp'), may hold values from 0.099609375 to 1.8984375
- w_gate: bfloat16 [960, 2560], P('fsdp', 'tp'), may hold values from -0.1875 to 0.1875
- w_up: bfloat16 [960, 2560], P('fsdp', 'tp'), may hold values from -0.1875 to 0.1875
- w_down: bfloat16 [960, 2560], P('fsdp', 'tp'), may hold values from -0.25 to 0.25
Outputs:
- result: bfloat16 [8, 2048, 960], P('fsdp', ('ctx', 'tp'))
- grad_tokens: float32 [8, 2048, 960], P('fsdp', ('ctx', 'tp'))
- grad_input_gain: float32 [960], P('fsdp')
- grad_w_query: float32 [960, 960], P('fsdp')
- grad_w_keyval: float32 [960, 640], P('fsdp')
- grad_w_output: float32 [960, 960], P('fsdp')
- grad_middle_gain: float32 [960], P('fsdp')
- grad_w_gate: float32 [960, 2560], P('fsdp', 'tp')
- grad_w_up: float32 [960, 2560], P('fsdp', 'tp')
- grad_w_down: float32 [960, 2560], P('fsdp', 'tp')
All inputs are finite; a program needn't handle non-finite values.
Results may differ from a plain program's by a relative error of at most 0.02.
Values may be sent and summed in bfloat16 or wider, within the bound.
A program may use at most 128 MiB of HBM per device.

v0:
```python
from functools import partial
import jax
import jax.numpy as jnp
from jax import lax
from jax.sharding import PartitionSpec as P

QUERY_HEADS = 15
KEYVAL_HEADS = 5
HEAD_WIDTH = 64
SEQUENCE_LENGTH = 2048
KEY_WIDTH = 320
EPS = 1e-05
THETA = 10000.0


def rope_tables(token_positions, first_place):
    half_width = HEAD_WIDTH // 2
    position = (first_place + lax.iota(jnp.int32, token_positions)).astype(jnp.float32)
    frequency = THETA ** (-(2.0 * lax.iota(jnp.int32, half_width).astype(jnp.float32)) / HEAD_WIDTH)
    angles = position[:, None] * frequency[None, :]
    return (jnp.cos(angles), jnp.sin(angles))


def apply_rotary(value_rows, cosine_table, sine_table, heads):
    half_width = HEAD_WIDTH // 2
    shaped = value_rows.reshape(value_rows.shape[:-1] + (heads, HEAD_WIDTH))
    leading = shaped[..., :half_width]
    trailing = shaped[..., half_width:]
    cosine_wide = cosine_table[:, None, :]
    sine_wide = sine_table[:, None, :]
    turned = jnp.concatenate(
        [
            leading * cosine_wide - trailing * sine_wide,
            trailing * cosine_wide + leading * sine_wide,
        ],
        -1,
    )
    return turned.reshape(value_rows.shape)


def normalize(value_rows):
    inverse_rms = lax.rsqrt(jnp.mean(value_rows * value_rows, -1, keepdims=True) + EPS)
    return (value_rows * inverse_rms, inverse_rms)


def norm_back(back_unit, unit_rows, inverse_rms):
    return inverse_rms * (
        back_unit - unit_rows * jnp.mean(back_unit * unit_rows, -1, keepdims=True)
    )


def to_heads(value_rows, sequence_count, token_positions):
    group_total = QUERY_HEADS // KEYVAL_HEADS
    return (
        value_rows.reshape(sequence_count, token_positions, KEYVAL_HEADS, group_total, HEAD_WIDTH)
        .transpose(0, 2, 3, 1, 4)
        .reshape(sequence_count * KEYVAL_HEADS, group_total * token_positions, HEAD_WIDTH)
    )


def from_heads(value_rows, sequence_count, token_positions):
    group_total = QUERY_HEADS // KEYVAL_HEADS
    return (
        value_rows.reshape(sequence_count, KEYVAL_HEADS, group_total, token_positions, HEAD_WIDTH)
        .transpose(0, 3, 1, 2, 4)
        .reshape(sequence_count, token_positions, QUERY_HEADS * HEAD_WIDTH)
    )


def per_sequence(value_rows, sequence_count):
    return value_rows.reshape((sequence_count, KEYVAL_HEADS) + value_rows.shape[1:])


def masked_scores(query_group, key_group, allowed):
    raw_scores = jnp.einsum("qd,kd->qk", query_group, key_group, preferred_element_type=jnp.float32)
    return jnp.where(allowed, raw_scores * HEAD_WIDTH ** (-0.5), -jnp.inf)


def head_forward(head_items, allowed):
    query_group, key_group, value_group = head_items
    scores = masked_scores(query_group, key_group, allowed)
    row_top = jnp.max(scores, -1, keepdims=True)
    lifted = jnp.exp(scores - row_top)
    row_total = jnp.sum(lifted, -1, keepdims=True)
    weights = (lifted / row_total).astype(jnp.bfloat16)
    mixed_heads = jnp.einsum("qk,kd->qd", weights, value_group, preferred_element_type=jnp.float32)
    return (mixed_heads, row_top[:, 0], row_total[:, 0])


def head_backward(head_items, allowed):
    query_group, key_group, value_group, back_mixed, row_top, row_total = head_items
    scores = masked_scores(query_group, key_group, allowed)
    weights = jnp.exp(scores - row_top[:, None]) / row_total[:, None]
    back_weights = jnp.einsum(
        "qd,kd->qk", back_mixed, value_group, preferred_element_type=jnp.float32
    )
    weighted_sum = jnp.sum(weights * back_weights, -1, keepdims=True)
    back_scores = (weights * (back_weights - weighted_sum)).astype(jnp.bfloat16)
    back_query = jnp.einsum(
        "qk,kd->qd", back_scores, key_group, preferred_element_type=jnp.float32
    ) * HEAD_WIDTH ** (-0.5)
    back_key = jnp.einsum(
        "qk,qd->kd", back_scores, query_group, preferred_element_type=jnp.float32
    ) * HEAD_WIDTH ** (-0.5)
    back_value = jnp.einsum(
        "qk,qd->kd", weights.astype(jnp.bfloat16), back_mixed, preferred_element_type=jnp.float32
    )
    return (back_query, back_key, back_value)


def on_device(
    tokens, cotangent, input_gain, w_query, w_keyval, w_output, middle_gain, w_gate, w_up, w_down
):
    sequence_count = tokens.shape[0]
    token_positions = tokens.shape[1]
    group_total = QUERY_HEADS // KEYVAL_HEADS
    place_index = lax.axis_index("ctx") * lax.axis_size("tp") + lax.axis_index("tp")
    first_place = place_index * token_positions
    cosine_table, sine_table = rope_tables(token_positions, first_place)
    query_place = first_place + lax.iota(jnp.int32, group_total * token_positions) % token_positions
    allowed = lax.iota(jnp.int32, SEQUENCE_LENGTH)[None, :] <= query_place[:, None]
    full_gain_one, full_query, full_keyval, full_output = (
        lax.all_gather(input_gain, "fsdp", axis=0, tiled=True),
        lax.all_gather(w_query, "fsdp", axis=0, tiled=True),
        lax.all_gather(w_keyval, "fsdp", axis=0, tiled=True),
        lax.all_gather(w_output, "fsdp", axis=0, tiled=True),
    )
    gain_one = full_gain_one.astype(jnp.float32)
    inputs = tokens.astype(jnp.float32)
    unit_one, inverse_one = normalize(inputs)
    normed_one = (unit_one * gain_one).astype(jnp.bfloat16)
    query_raw = jnp.dot(normed_one, full_query, preferred_element_type=jnp.float32)
    keyval_unrotated = jnp.dot(normed_one, full_keyval, preferred_element_type=jnp.float32)
    query_low = apply_rotary(query_raw, cosine_table, sine_table, QUERY_HEADS).astype(jnp.bfloat16)
    keyval_low = jnp.concatenate(
        [
            apply_rotary(keyval_unrotated[..., :KEY_WIDTH], cosine_table, sine_table, KEYVAL_HEADS),
            keyval_unrotated[..., KEY_WIDTH:],
        ],
        -1,
    ).astype(jnp.bfloat16)
    keyval_gathered = lax.all_gather(keyval_low, ("ctx", "tp"), axis=1, tiled=True)
    query_heads = to_heads(query_low, sequence_count, token_positions)
    stacked = (
        keyval_gathered.reshape(sequence_count, SEQUENCE_LENGTH, 2, KEYVAL_HEADS, HEAD_WIDTH)
        .transpose(2, 0, 3, 1, 4)
        .reshape(2, sequence_count * KEYVAL_HEADS, SEQUENCE_LENGTH, HEAD_WIDTH)
    )
    key_heads = stacked[0]
    value_heads = stacked[1]
    mixed_heads, row_top, row_total = lax.map(
        partial(head_forward, allowed=allowed), (query_heads, key_heads, value_heads)
    )
    mixed_low = from_heads(mixed_heads, sequence_count, token_positions).astype(jnp.bfloat16)
    attention_out = jnp.dot(mixed_low, full_output, preferred_element_type=jnp.float32)
    middle = inputs + attention_out
    full_gate, full_up, full_down, full_gain_two = (
        lax.all_gather(w_gate, "fsdp", axis=0, tiled=True),
        lax.all_gather(w_up, "fsdp", axis=0, tiled=True),
        lax.all_gather(w_down, "fsdp", axis=0, tiled=True),
        lax.all_gather(middle_gain, "fsdp", axis=0, tiled=True),
    )
    gain_two = full_gain_two.astype(jnp.float32)
    unit_two, inverse_two = normalize(middle)
    normed_two = (unit_two * gain_two).astype(jnp.bfloat16)
    pair_rows, pair_cotangent = (
        lax.all_gather(normed_two, "tp", axis=1, tiled=True),
        lax.all_gather(cotangent, "tp", axis=1, tiled=True),
    )
    gate_proj = jnp.dot(pair_rows, full_gate, preferred_element_type=jnp.float32)
    up_proj = jnp.dot(pair_rows, full_up, preferred_element_type=jnp.float32)
    sigmoid_gate = jax.nn.sigmoid(gate_proj)
    swish_gate = gate_proj * sigmoid_gate
    hidden = (swish_gate * up_proj).astype(jnp.bfloat16)
    branch_part = jnp.einsum("spf,df->spd", hidden, full_down, preferred_element_type=jnp.float32)
    feed_out = lax.psum_scatter(
        branch_part.astype(jnp.bfloat16), "tp", scatter_dimension=1, tiled=True
    ).astype(jnp.float32)
    result = (middle + feed_out).astype(jnp.bfloat16)
    back_hidden = jnp.dot(pair_cotangent, full_down, preferred_element_type=jnp.float32)
    back_gate = (
        back_hidden * up_proj * sigmoid_gate * (1.0 + gate_proj * (1.0 - sigmoid_gate))
    ).astype(jnp.bfloat16)
    back_up = (back_hidden * swish_gate).astype(jnp.bfloat16)
    grad_down = jnp.einsum(
        "spd,spf->df", pair_cotangent, hidden, preferred_element_type=jnp.float32
    )
    grad_gate = jnp.einsum("spd,spf->df", pair_rows, back_gate, preferred_element_type=jnp.float32)
    grad_up = jnp.einsum("spd,spf->df", pair_rows, back_up, preferred_element_type=jnp.float32)
    back_normed_part = jnp.einsum(
        "spf,df->spd", back_gate, full_gate, preferred_element_type=jnp.float32
    ) + jnp.einsum("spf,df->spd", back_up, full_up, preferred_element_type=jnp.float32)
    back_normed_two = lax.psum_scatter(back_normed_part, "tp", scatter_dimension=1, tiled=True)
    grad_gain_two = jnp.sum(back_normed_two * unit_two, axis=(0, 1))
    back_middle = cotangent.astype(jnp.float32) + norm_back(
        back_normed_two * gain_two, unit_two, inverse_two
    )
    back_attention = back_middle.astype(jnp.bfloat16)
    grad_output = jnp.einsum(
        "spq,spd->qd", mixed_low, back_attention, preferred_element_type=jnp.float32
    )
    back_mixed = jnp.einsum(
        "spd,qd->spq", back_attention, full_output, preferred_element_type=jnp.float32
    ).astype(jnp.bfloat16)

    def attend_back(carried, sequence_items):
        back_query, back_key, back_value = lax.map(
            partial(head_backward, allowed=allowed), sequence_items
        )
        back_keyval = (
            jnp.stack([back_key, back_value])
            .transpose(2, 0, 1, 3)
            .reshape(SEQUENCE_LENGTH, 2 * KEY_WIDTH)
        )
        owned_rows = lax.psum_scatter(
            back_keyval.astype(jnp.bfloat16), ("ctx", "tp"), scatter_dimension=0, tiled=True
        ).astype(jnp.float32)
        return (carried, (back_query, owned_rows))

    sequence_items = tuple(
        (
            per_sequence(value_rows, sequence_count)
            for value_rows in (
                query_heads,
                key_heads,
                value_heads,
                to_heads(back_mixed, sequence_count, token_positions),
                row_top,
                row_total,
            )
        )
    )
    unused, (query_gradient_full, owned_tokens_full) = lax.scan(
        attend_back, jnp.zeros((), jnp.float32), sequence_items
    )
    back_query_rows = from_heads(
        query_gradient_full.reshape(
            (sequence_count * KEYVAL_HEADS,) + query_gradient_full.shape[2:]
        ),
        sequence_count,
        token_positions,
    )
    back_query_low = apply_rotary(back_query_rows, cosine_table, -sine_table, QUERY_HEADS).astype(
        jnp.bfloat16
    )
    back_keyval_low = jnp.concatenate(
        [
            apply_rotary(
                owned_tokens_full[..., :KEY_WIDTH], cosine_table, -sine_table, KEYVAL_HEADS
            ),
            owned_tokens_full[..., KEY_WIDTH:],
        ],
        -1,
    ).astype(jnp.bfloat16)
    grad_query = jnp.einsum(
        "spd,spq->dq", normed_one, back_query_low, preferred_element_type=jnp.float32
    )
    grad_keyval = jnp.einsum(
        "spd,spk->dk", normed_one, back_keyval_low, preferred_element_type=jnp.float32
    )
    back_normed_one = jnp.einsum(
        "spq,dq->spd", back_query_low, full_query, preferred_element_type=jnp.float32
    ) + jnp.einsum("spk,dk->spd", back_keyval_low, full_keyval, preferred_element_type=jnp.float32)
    grad_gain_one = jnp.sum(back_normed_one * unit_one, axis=(0, 1))
    back_inputs = back_middle + norm_back(back_normed_one * gain_one, unit_one, inverse_one)
    attention_term = jnp.concatenate([grad_query, grad_keyval, grad_output], 1)
    feed_term = jnp.concatenate([grad_gate, grad_up, grad_down], 1)
    attention_total, gain_one_total, gain_two_total = (
        lax.psum(attention_term.astype(jnp.bfloat16), ("ctx", "tp")).astype(jnp.float32),
        lax.psum(grad_gain_one.astype(jnp.bfloat16), ("ctx", "tp")).astype(jnp.float32),
        lax.psum(grad_gain_two.astype(jnp.bfloat16), ("ctx", "tp")).astype(jnp.float32),
    )
    feed_total = lax.psum(feed_term.astype(jnp.bfloat16), "ctx")
    attention_share, feed_share, gain_one_share, gain_two_share = (
        lax.psum_scatter(
            attention_total.astype(jnp.bfloat16), "fsdp", scatter_dimension=0, tiled=True
        ).astype(jnp.float32),
        lax.psum_scatter(feed_total, "fsdp", scatter_dimension=0, tiled=True).astype(jnp.float32),
        lax.psum_scatter(
            gain_one_total.astype(jnp.bfloat16), "fsdp", scatter_dimension=0, tiled=True
        ).astype(jnp.float32),
        lax.psum_scatter(
            gain_two_total.astype(jnp.bfloat16), "fsdp", scatter_dimension=0, tiled=True
        ).astype(jnp.float32),
    )
    query_width = full_query.shape[1]
    keyval_width = full_keyval.shape[1]
    hidden_width = full_gate.shape[1]
    share_query = attention_share[:, :query_width]
    share_keyval = attention_share[:, query_width : query_width + keyval_width]
    share_output = attention_share[:, query_width + keyval_width :]
    share_gate = feed_share[:, :hidden_width]
    share_up = feed_share[:, hidden_width : 2 * hidden_width]
    share_down = feed_share[:, 2 * hidden_width :]
    return (
        result,
        back_inputs,
        gain_one_share,
        share_query,
        share_keyval,
        share_output,
        gain_two_share,
        share_gate,
        share_up,
        share_down,
    )


def solution(mesh):
    in_specs = (
        P("fsdp", ("ctx", "tp"), None),
        P("fsdp", ("ctx", "tp"), None),
        P("fsdp"),
        P("fsdp", None),
        P("fsdp", None),
        P("fsdp", None),
        P("fsdp"),
        P("fsdp", "tp"),
        P("fsdp", "tp"),
        P("fsdp", "tp"),
    )
    out_specs = (
        P("fsdp", ("ctx", "tp"), None),
        P("fsdp", ("ctx", "tp"), None),
        P("fsdp"),
        P("fsdp", None),
        P("fsdp", None),
        P("fsdp", None),
        P("fsdp"),
        P("fsdp", "tp"),
        P("fsdp", "tp"),
        P("fsdp", "tp"),
    )
    return jax.shard_map(
        on_device, mesh=mesh, in_specs=in_specs, out_specs=out_specs, check_vma=False
    )
```

profile of v0, /device:TPU:0, one launch (start us, length us, event | category | flops | bytes accessed | tf_op | source)
XLA Modules:
  0.0 1055.6 jit_solution(356635097389830232)
XLA Ops:
  12.4 8.3 all-reduce.6
  23.0 7.0 all-gather.12.cloned.1.call-done
  37.5 16.0 %all-gather.10.cloned.1.call-done = bf16[960,960]{1,0:T(8,128)(2,1)} async-done(((bf16[240,960]{1,0:T(8,128)(2,1)}), bf16[960,960]{1,0:T(8,128)(2,1)}) %all-gather.10.cloned.1.call-update) | async-done | bytes 1843216 | tf_op jit(solution)/shard_map/all_gather | solution.py:124
  58.6 84.0 %all-gather.14.cloned.1.call-done = bf16[2,2048,640]{2,1,0:T(8,128)(2,1)} async-done(((bf16[2,256,640]{2,1,0:T(8,128)(2,1)}), bf16[2,2048,640]{2,1,0:T(8,128)(2,1)}) %all-gather.14.cloned.1.call-update) | async-done | bytes 5242896 | tf_op jit(solution)/shard_map/all_gather | solution.py:142
  142.6 8.0 copy.72
  150.6 7.3 slice_bitcast_fusion
  157.9 80.6 %while.43 = (s32[]{:T(128)}, bf16[10,768,64]{1,2,0:T(8,128)(2,1)S(1)}, f32[10,768]{1,0:T(8,128)S(1)}, f32[10,768]{1,0:T(8,128)S(1)}, bf16[10,768,64]{2,1,0:T(8,1...) while((s32[]{:T(128)}, ...), condition=%wide.region_4.5_spmd.clone, body=%wide.region_1.4_spmd.clone.sunk | while | flops 426244608 | bytes 19846260 | solution.py:151
  162.3 3.3 fusion.152
  170.4 3.4 fusion.152
  178.5 3.3 fusion.152
  186.5 3.3 fusion.152
  194.5 3.3 fusion.152
  202.6 3.3 fusion.152
  210.7 3.4 fusion.152
  218.8 3.3 fusion.152
  226.8 3.3 fusion.152
  234.9 3.3 fusion.152
  243.4 3.1 multiply_reduce_fusion.3
  248.7 7.6 fusion.58
  256.3 26.9 %all-gather.18.cloned.1.call-done = bf16[2,512,960]{1,2,0:T(8,128)(2,1)} async-done(((bf16[2,256,960]{1,2,0:T(8,128)(2,1)}), bf16[2,512,960]{1,2,0:T(8,128)(2,1)}) %all-gather.18.cloned.1.call-update) | async-done | bytes 1966096 | tf_op jit(solution)/shard_map/all_gather | solution.py:167
  283.1 7.6 fusion.64
  290.7 18.6 %all-gather.20.cloned.1.call-done = bf16[960,1280]{1,0:T(8,128)(2,1)} async-done(((bf16[240,1280]{1,0:T(8,128)(2,1)}), bf16[960,1280]{1,0:T(8,128)(2,1)}) %all-gather.20.cloned.1.call-update) | async-done | bytes 2457616 | tf_op jit(solution)/shard_map/all_gather | solution.py:158
  309.4 11.9 %multiply_convert_fusion.2 = (bf16[2,512,1280]{2,1,0:T(8,128)(2,1)S(1)}, bf16[2,512,1280]{2,1,0:T(8,128)(2,1)S(1)}, bf16[2,512,1280]{2,1,0:T(8,128)(2,1)}) fusion(f32[2,512,1280]{2,1,0:T(8,128)} %fusion.58, f32[2,512,1280]{2,1,0:T(8,128)} %fusion.64, bf16[2,512,960]{1,2,0:T(8,128)(2,1)} %all-gather.18.cloned.1.call-done, ...), kind=kOutput, calls=%fused_computation.71 | convolution fusion | flops 2536243200 | bytes 22773760 | tf_op jit(solution)/shard_map/dot_general | solution.py:170
  324.8 4.9 fusion.85
  329.8 6.5 fusion.88
  336.4 5.6 fusion.53
  342.0 3.4 bitcast_convert_fusion.2
  345.4 3.4 bitcast_convert_fusion.1
  348.9 3.4 pad_maximum_fusion.1
  352.3 29.6 %reduce-scatter.8.cloned.1.call-done = f32[2,256,960]{1,2,0:T(8,128)} async-done(((f32[2,512,960]{1,2,0:T(8,128)}), f32[2,256,960]{1,2,0:T(8,128)}) %reduce-scatter.8.cloned.1.call-update) | async-done | bytes 1966096 | tf_op jit(solution)/shard_map/reduce_scatter | solution.py:193
  384.5 30.1 %reduce-scatter.6.cloned.1.call-done = bf16[2,256,960]{1,2,0:T(8,128)(2,1)} async-done(((bf16[2,512,960]{1,2,0:T(8,128)(2,1)}), bf16[2,256,960]{1,2,0:T(8,128)(2,1)}) %reduce-scatter.6.cloned.1.call-update) | async-done | bytes 983056 | tf_op jit(solution)/shard_map/reduce_scatter | solution.py:176
  414.6 3.5 multiply_add_fusion
  421.2 340.2 %while.45 = (s32[]{:T(128)}, f32[2,5,768,64]{2,3,1,0:T(8,128)}, f32[2,256,640]{1,2,0:T(8,128)}, bf16[2,5,768,64]{3,2,1,0:T(8,128)(2,1)}, bf16[2,5,2048,64]{2,3,1...) while((s32[]{:T(128)}, f32[2,5,768,64]{2,3,1,0:T(8,128)}, ...), condition=%wide.region_14.15_spmd.clone, body=%wide.region_9.14_spmd.clone.sunk | while | flops 1025588480 | bytes 125203080 | solution.py:233
  423.8 3.0 constant_dynamic-slice_fusion.3
  429.5 3.1 copy.95
  435.6 79.8 %while.46 = (s32[]{:T(128)}, f32[5,768,64]{1,2,0:T(8,128)}, bf16[5,2048,64]{1,2,0:T(8,128)(2,1)}, bf16[5,2048,64]{1,2,0:T(8,128)(2,1)}, bf16[5,768,64]{2,1,0:T(8...) while((s32[]{:T(128)}, f32[5,768,64]{1,2,0:T(8,128)}, ...), condition=%wide.region_12.12_spmd, body=%wide.region_10.11_spmd.sunk | while | flops 1022541056 | bytes 79656208 | solution.py:207
  439.1 3.7 multiply_reduce_fusion.5
  455.1 3.7 multiply_reduce_fusion.5
  471.1 3.7 multiply_reduce_fusion.5
  487.0 3.7 multiply_reduce_fusion.5
  503.0 3.7 multiply_reduce_fusion.5
  515.4 3.5 pad_maximum_fusion.11
  521.2 68.9 %reduce-scatter.14.cloned.1.call-done = bf16[256,640]{0,1:T(8,128)(2,1)} async-done(((bf16[2048,640]{0,1:T(8,128)(2,1)}), bf16[256,640]{0,1:T(8,128)(2,1)}) %reduce-scatter.14.cloned.1.call-update) | async-done | bytes 327696 | tf_op jit(solution)/shard_map/while/body/eval_jaxpr/reduce_scatter | solution.py:215
  594.4 3.0 constant_dynamic-slice_fusion.3
  600.1 3.1 copy.95
  606.1 79.8 %while.46 = (s32[]{:T(128)}, f32[5,768,64]{1,2,0:T(8,128)}, bf16[5,2048,64]{1,2,0:T(8,128)(2,1)}, bf16[5,2048,64]{1,2,0:T(8,128)(2,1)}, bf16[5,768,64]{2,1,0:T(8...) while((s32[]{:T(128)}, f32[5,768,64]{1,2,0:T(8,128)}, ...), condition=%wide.region_12.12_spmd, body=%wide.region_10.11_spmd.sunk | while | flops 1022541056 | bytes 79656208 | solution.py:207
  609.7 3.7 multiply_reduce_fusion.5
  625.6 3.7 multiply_reduce_fusion.5
  641.6 3.7 multiply_reduce_fusion.5
  657.6 3.7 multiply_reduce_fusion.5
  673.5 3.7 multiply_reduce_fusion.5
  686.0 3.5 pad_maximum_fusion.11
  691.8 67.5 %reduce-scatter.14.cloned.1.call-done = bf16[256,640]{0,1:T(8,128)(2,1)} async-done(((bf16[2048,640]{0,1:T(8,128)(2,1)}), bf16[256,640]{0,1:T(8,128)(2,1)}) %reduce-scatter.14.cloned.1.call-update) | async-done | bytes 327696 | tf_op jit(solution)/shard_map/while/body/eval_jaxpr/reduce_scatter | solution.py:215
  763.8 3.1 reshape_reshape.14
  779.7 9.3 concatenate.38
  789.1 40.0 %reduce-scatter.12.cloned.1.call-done = bf16[240,3840]{1,0:T(8,128)(2,1)} async-done(((bf16[960,3840]{1,0:T(8,128)(2,1)}), bf16[240,3840]{1,0:T(8,128)(2,1)}) %reduce-scatter.12.cloned.1.call-update) | async-done | bytes 1843216 | tf_op jit(solution)/shard_map/reduce_scatter | solution.py:278
  829.9 3.1 fusion.81
  835.5 5.7 all-reduce.5
  841.4 21.5 %all-reduce.4 = (bf16[240]{0:T(256)(128)(2,1)S(1)}, bf16[240]{0:T(256)(128)(2,1)S(1)}) all-reduce(bf16[240]{0:T(256)(128)(2,1)S(1)} %dynamic-slice.3, bf16[240]{0:T(256)(128)(2,1)S(1)} %dynamic-slice.5), channel_id=1, replica_groups=mesh['fsdp'=4,'ctx'=4,'tp'=2] {'ctx','tp'}, use_global_device_ids=true, to_apply=%region_17.18 | all-reduce | flops 480 | bytes 1920 | tf_op jit(solution)/shard_map/psum | solution.py:270
  864.1 16.8 %reduce-scatter.10.cloned.1.call-done = bf16[240,2560]{1,0:T(8,128)(2,1)} async-done(((bf16[960,2560]{1,0:T(8,128)(2,1)}), bf16[240,2560]{1,0:T(8,128)(2,1)}) %reduce-scatter.10.cloned.1.call-update) | async-done | bytes 1228816 | tf_op jit(solution)/shard_map/reduce_scatter | solution.py:275
  881.0 3.3 fusion.74
  884.3 77.4 %all-reduce.12.cloned.1.call-done = bf16[240,3840]{1,0:T(8,128)(2,1)} async-done(((bf16[240,3840]{1,0:T(8,128)(2,1)}), bf16[240,3840]{1,0:T(8,128)(2,1)}) %all-reduce.12.cloned.1.call-update) | async-done | bytes 1843216 | tf_op jit(solution)/shard_map/psum | solution.py:273
  961.7 3.4 fusion.112
  965.0 80.2 %all-reduce.10.cloned.1.call-done = bf16[240,2560]{1,0:T(8,128)(2,1)} async-done(((bf16[240,2560]{1,0:T(8,128)(2,1)}), bf16[240,2560]{1,0:T(8,128)(2,1)}) %all-reduce.10.cloned.1.call-update) | async-done | bytes 1228816 | tf_op jit(solution)/shard_map/psum | solution.py:269
  (417 shorter events, 251.3 us)
Async XLA Ops:
  7.2 22.9 %copy-start.11 = (bf16[2,256,960]{1,2,0:T(8,128)(2,1)S(1)}, bf16[2,256,960]{1,2,0:T(8,128)(2,1)}, u32[]{:S(2)}) copy-start(bf16[2,256,960]{1,2,0:T(8,128)(2,1)} %param.16) | copy-start | bytes 2949124
  7.2 22.9 %all-gather.12.cloned.1.call-start = ((), (), s32[]{:S(2)}) async-start(), calls=%async_computation.6 | async-start | bytes 1536000 | tf_op jit(solution)/shard_map/all_gather | solution.py:125
  7.9 45.6 %all-gather.10.cloned.1.call-start = ((), (), s32[]{:S(2)}) async-start(), calls=%async_computation.5 | async-start | bytes 2457600 | tf_op jit(solution)/shard_map/all_gather | solution.py:124
  8.7 133.9 %all-gather.14.cloned.1.call-start = ((), (), s32[]{:S(2)}) async-start(), calls=%async_computation.7 | async-start | bytes 5898240 | tf_op jit(solution)/shard_map/all_gather | solution.py:142
  20.8 32.8 %copy-start.28 = (f32[960]{0:T(1024)}, f32[960]{0:T(1024)S(1)}, u32[]{:S(2)}) copy-start(f32[960]{0:T(1024)S(1)} %convert_element_type.123) | copy-start | bytes 11524
  22.2 31.3 %copy-start.31 = (f32[2,256]{1,0:T(2,128)}, f32[2,256]{1,0:T(2,128)S(1)}, u32[]{:S(2)}) copy-start(f32[2,256]{1,0:T(2,128)S(1)} %add_rsqrt_fusion.1) | copy-start | bytes 6148
  23.0 33.4 %copy-start.21 = (f32[256,32]{0,1:T(8,128)}, f32[256,32]{0,1:T(8,128)S(1)}, u32[]{:S(2)}) copy-start(f32[256,32]{0,1:T(8,128)S(1)} %get-tuple-element.374) | copy-start | bytes 98308
  34.4 208.9 %all-gather.16.cloned.1.call-start = ((), (), s32[]{:S(2)}) async-start(), calls=%async_computation.8 | async-start | bytes 2457600 | tf_op jit(solution)/shard_map/all_gather | solution.py:126
  35.0 213.7 %all-gather.26.cloned.1.call-start = ((), (), s32[]{:S(2)}) async-start(), calls=%async_computation.14 | async-start | bytes 2949120 | tf_op jit(solution)/shard_map/all_gather | solution.py:168
  35.6 213.1 %all-gather.24.cloned.1.call-start = ((), (), s32[]{:S(2)}) async-start(), calls=%async_computation.12 | async-start | bytes 3072000 | tf_op jit(solution)/shard_map/all_gather | solution.py:160
  36.2 220.1 %all-gather.22.cloned.1.call-start = ((), (), s32[]{:S(2)}) async-start(), calls=%async_computation.11 | async-start | bytes 3072000 | tf_op jit(solution)/shard_map/all_gather | solution.py:159
  36.9 246.2 %all-gather.18.cloned.1.call-start = ((), (), s32[]{:S(2)}) async-start(), calls=%async_computation.9 | async-start | bytes 2949120 | tf_op jit(solution)/shard_map/all_gather | solution.py:167
  150.6 7.3 copy-start.18
  247.7 61.7 %all-gather.20.cloned.1.call-start = ((), (), s32[]{:S(2)}) async-start(), calls=%async_computation.10 | async-start | bytes 3072000 | tf_op jit(solution)/shard_map/all_gather | solution.py:158
  248.5 133.4 %reduce-scatter.8.cloned.1.call-start = ((), (), s32[]{:S(2)}) async-start(), calls=%async_computation.15 | async-start | bytes 5898240 | tf_op jit(solution)/shard_map/reduce_scatter | solution.py:193
  309.4 11.9 %copy-start.33 = (bf16[960,1280]{1,0:T(8,128)(2,1)S(1)}, bf16[960,1280]{1,0:T(8,128)(2,1)}, u32[]{:S(2)}) copy-start(bf16[960,1280]{1,0:T(8,128)(2,1)} %all-gather.22.cloned.1.call-done) | copy-start | bytes 7372804
  321.3 2.8 copy-start.38
  321.3 2.8 copy-start.40
  321.3 3.5 copy-start.34
  329.7 84.9 %reduce-scatter.6.cloned.1.call-start = ((), (), s32[]{:S(2)}) async-start(), calls=%async_computation.13 | async-start | bytes 2949120 | tf_op jit(solution)/shard_map/reduce_scatter | solution.py:176
  336.4 5.6 copy-start.36
  336.4 5.6 copy-start.41
  342.0 3.5 copy-start.39
  352.2 62.4 %copy-start.10 = (bf16[2,256,960]{1,2,0:T(8,128)(2,1)S(1)}, bf16[2,256,960]{1,2,0:T(8,128)(2,1)}, u32[]{:S(2)}) copy-start(bf16[2,256,960]{1,2,0:T(8,128)(2,1)} %param.17) | copy-start | bytes 2949124
  414.6 3.5 copy-start.35
  421.6 168.5 %reduce-scatter.14.cloned.1.call-start = ((), (), s32[]{:S(2)}) async-start(), calls=%async_computation.20 | async-start | bytes 2949120 | tf_op jit(solution)/shard_map/while/body/eval_jaxpr/reduce_scatter | solution.py:215
  445.8 2.9 copy-start.3
  448.7 2.8 copy-start.1
  461.7 2.9 copy-start.3
  464.7 2.8 copy-start.1
  477.7 2.9 copy-start.3
  480.6 2.8 copy-start.1
  493.7 2.9 copy-start.3
  496.6 2.9 copy-start.1
  509.7 2.9 copy-start.3
  512.6 2.8 copy-start.1
  519.0 71.1 %copy-start.13 = (f32[2,256,640]{1,2,0:T(8,128)S(1)}, f32[2,256,640]{1,2,0:T(8,128)}, u32[]{:S(2)}) copy-start(f32[2,256,640]{1,2,0:T(8,128)} %get-tuple-element.691) | copy-start | bytes 3932164 | tf_op jit(solution)/shard_map/while
  592.2 167.1 %reduce-scatter.14.cloned.1.call-start = ((), (), s32[]{:S(2)}) async-start(), calls=%async_computation.20 | async-start | bytes 2949120 | tf_op jit(solution)/shard_map/while/body/eval_jaxpr/reduce_scatter | solution.py:215
  616.3 2.9 copy-start.3
  619.3 2.9 copy-start.1
  632.3 2.9 copy-start.3
  635.2 2.8 copy-start.1
  648.2 2.9 copy-start.3
  651.2 2.8 copy-start.1
  664.2 2.9 copy-start.3
  667.1 2.9 copy-start.1
  680.2 2.9 copy-start.3
  683.1 2.8 copy-start.1
  689.5 69.8 %copy-start.13 = (f32[2,256,640]{1,2,0:T(8,128)S(1)}, f32[2,256,640]{1,2,0:T(8,128)}, u32[]{:S(2)}) copy-start(f32[2,256,640]{1,2,0:T(8,128)} %get-tuple-element.691) | copy-start | bytes 3932164 | tf_op jit(solution)/shard_map/while
  761.4 67.7 %reduce-scatter.12.cloned.1.call-start = ((), (), s32[]{:S(2)}) async-start(), calls=%async_computation.18 | async-start | bytes 9216000 | tf_op jit(solution)/shard_map/reduce_scatter | solution.py:278
  761.9 119.0 %reduce-scatter.10.cloned.1.call-start = ((), (), s32[]{:S(2)}) async-start(), calls=%async_computation.16 | async-start | bytes 6144000 | tf_op jit(solution)/shard_map/reduce_scatter | solution.py:275
  766.9 2.6 copy-start.22
  766.9 2.6 copy-start.27
  768.6 2.2 copy-start.8
  772.6 2.1 copy-start.20
  774.7 2.5 copy-start.7
  774.7 2.5 copy-start.17
  789.0 172.6 %all-reduce.12.cloned.1.call-start = ((), (), s32[]{:S(2)}) async-start(), calls=%async_computation.19 | async-start | bytes 3686400 | tf_op jit(solution)/shard_map/psum | solution.py:273
  829.1 216.1 %all-reduce.10.cloned.1.call-start = ((), (), s32[]{:S(2)}) async-start(), calls=%async_computation.17 | async-start | bytes 2457600 | tf_op jit(solution)/shard_map/psum | solution.py:269
  829.8 3.2 copy-start.24
  829.8 3.1 copy-start.26
  829.8 3.1 copy-start.37
  833.0 2.5 copy-start.30
  1045.3 2.1 copy-start.9
  (43 other events, 64.0 us)
Sparse Core Ops, SparseCore 0:
  9.6 20.4 all-gather.11
  31.6 21.8 all-gather.9
  56.3 86.2 all-gather.13
  144.0 20.0 all-gather.15
  165.4 31.5 all-gather.25
  198.5 24.6 all-gather.23
  224.8 24.5 all-gather.21
  251.5 31.5 all-gather.17
  284.7 24.6 all-gather.19
  329.8 51.9 reduce-scatter.7
  384.2 30.3 reduce-scatter.5
  519.1 70.9 reduce-scatter.13
  689.7 69.5 reduce-scatter.13
  764.4 64.6 reduce-scatter.11
  831.7 49.1 reduce-scatter.9
  883.2 78.4 all-reduce.11
  965.0 80.1 all-reduce.9
where the time goes:
time: 1060 us
  waiting for transfers between devices  568 us (54%)
  matrix products  260 us (25%)
  local copies, waits for them, and re-layouts  112 us (11%)
  other arithmetic  60.4 us (6%)
  blocking collectives  35.6 us (3%)
  between operations  16 us (2%)
    reduce_scatter x2, waiting for transfers between devices, attend_back(): lax.psum_scatter(back_keyval.astype(jnp.bfloat16), ('ctx', 'tp'), scatter...  136 us
    all_gather x1, waiting for transfers between devices, on_device(): lax.all_gather(keyval_low, ('ctx', 'tp'), axis=1, tiled=True)  84 us
    psum x1, waiting for transfers between devices, on_device(): lax.psum(attention_term.astype(jnp.bfloat16), ('ctx', 'tp'))  80.2 us
    psum x1, waiting for transfers between devices, on_device(): feed_total = lax.psum(feed_term.astype(jnp.bfloat16), 'ctx')  77.4 us
    dot_general x20, matrix products, masked_scores(): jnp.einsum('qd,kd->qk', query_group, key_group, preferred_element_type=jn...  60.3 us
    reduce_scatter x1, waiting for transfers between devices, on_device(): lax.psum_scatter(feed_total, 'fsdp', scatter_dimension=0, tiled=True)  40 us
    dot_general x10, matrix products, head_forward(): jnp.einsum('qk,kd->qd', weights, value_group, preferred_element_type=jnp....  33.4 us
    reduce_scatter x1, waiting for transfers between devices, on_device(): lax.psum_scatter(branch_part.astype(jnp.bfloat16), 'tp', scatter_dimensio...  30.1 us
  transfers between devices with their start and end apart: 17, of which 13 were waited for; matrix products, arithmetic and copies ran while one was open for 19% of the time, Pallas kernels for 0%

commit v1 on v0

--- a/solution.py
+++ b/solution.py
@@ -139,7 +139,31 @@
         ],
         -1,
     ).astype(jnp.bfloat16)
-    keyval_gathered = lax.all_gather(keyval_low, ("ctx", "tp"), axis=1, tiled=True)
+    length, place, width = (
+        lax.axis_size(("ctx", "tp")),
+        lax.axis_index(("ctx", "tp")),
+        keyval_low.shape[1],
+    )
+    right = [(i, (i + 1) % length) for i in range(length)]
+    left = [(i, (i - 1) % length) for i in range(length)]
+    keyval_gathered = jnp.zeros(
+        (*keyval_low.shape[:1], length * width, *keyval_low.shape[1 + 1 :]), keyval_low.dtype
+    )
+    keyval_gathered = lax.dynamic_update_slice_in_dim(
+        keyval_gathered, keyval_low, place * width, axis=1
+    )
+    from_left = from_right = keyval_low
+    half = length // 2
+    for step in range(1, half + 1):
+        from_left = lax.ppermute(from_left, ("ctx", "tp"), right)
+        keyval_gathered = lax.dynamic_update_slice_in_dim(
+            keyval_gathered, from_left, (place - step) % length * width, axis=1
+        )
+        if step < length - half:
+            from_right = lax.ppermute(from_right, ("ctx", "tp"), left)
+            keyval_gathered = lax.dynamic_update_slice_in_dim(
+                keyval_gathered, from_right, (place + step) % length * width, axis=1
+            )
     query_heads = to_heads(query_low, sequence_count, token_positions)
     stacked = (
         keyval_gathered.reshape(sequence_count, SEQUENCE_LENGTH, 2, KEYVAL_HEADS, HEAD_WIDTH)

time: 1060 us -> 1070 us (level)
  starting transfers between devices: 1.31 us -> 16.1 us
  waiting for transfers between devices: 568 us -> 554 us
    ppermute x0 -> x7, waiting for transfers between devices: none -> 91 us  [the longest x4 88.3 us: on_device(): from_left = lax.ppermute(from_left, ('ctx', 'tp'), right)]
    all_gather x1 -> x0, waiting for transfers between devices: 84 us -> none  [on_device(): lax.all_gather(keyval_low, ('ctx', 'tp'), axis=1, tiled=True)]
    all_gather x1, waiting for transfers between devices: 16 us -> 0.01 us  [on_device(): lax.all_gather(w_query, 'fsdp', axis=0, tiled=True)]
    ppermute x0 -> x7, starting transfers between devices: none -> 15.3 us  [the longest x4 9.22 us: on_device(): from_left = lax.ppermute(from_left, ('ctx', 'tp'), right)]
  transfers between devices with their start and end apart: 17 -> 23, of which waited for: 13 -> 16; matrix products, arithmetic and copies ran while one was open for 19% -> 19% of each run, Pallas kernels for 0% -> 0%
where the time goes in v1:
time: 1070 us; the launch traced here: 1060 us
  waiting for transfers between devices  554 us (52%)
  matrix products  260 us (24%)
  local copies, waits for them, and re-layouts  121 us (11%)
  other arithmetic  58.3 us (5%)
  blocking collectives  35.6 us (3%)
  between operations  16.3 us (2%)
  starting transfers between devices  16.1 us (2%)
    reduce_scatter x2, waiting for transfers between devices, attend_back(): lax.psum_scatter(back_keyval.astype(jnp.bfloat16), ('ctx', 'tp'), scatter...  137 us
    ppermute x4, waiting for transfers between devices, on_device(): from_left = lax.ppermute(from_left, ('ctx', 'tp'), right)  88.3 us
    psum x1, waiting for transfers between devices, on_device(): lax.psum(attention_term.astype(jnp.bfloat16), ('ctx', 'tp'))  80.3 us
    psum x1, waiting for transfers between devices, on_device(): feed_total = lax.psum(feed_term.astype(jnp.bfloat16), 'ctx')  77.4 us
    dot_general x20, matrix products, masked_scores(): jnp.einsum('qd,kd->qk', query_group, key_group, preferred_element_type=jn...  60.1 us
    reduce_scatter x1, waiting for transfers between devices, on_device(): lax.psum_scatter(feed_total, 'fsdp', scatter_dimension=0, tiled=True)  40.3 us
    dot_general x10, matrix products, head_forward(): jnp.einsum('qk,kd->qd', weights, value_group, preferred_element_type=jnp....  33.4 us
    reduce_scatter x1, waiting for transfers between devices, on_device(): lax.psum_scatter(branch_part.astype(jnp.bfloat16), 'tp', scatter_dimensio...  29.9 us
  transfers between devices with their start and end apart: 23, of which 16 were waited for; matrix products, arithmetic and copies ran while one was open for 19% of the time, Pallas kernels for 0%

profile of v1, /device:TPU:0, one launch (start us, length us, event | category | flops | bytes accessed | tf_op | source)
XLA Modules:
  0.0 1063.4 jit_solution(17360830257828506106)
XLA Ops:
  12.4 8.3 all-reduce.6
  21.9 8.2 all-gather.11.cloned.1.call-done
  35.1 3.3 collective-permute-start.1
  38.4 25.2 %collective-permute-done = bf16[2,256,640]{2,1,0:T(8,128)(2,1)} collective-permute-done((bf16[2,256,640]{2,1,0:T(8,128)(2,1)S(1)}, bf16[2,256,640]{2,1,0:T(8,128)(2,1)}, u32[]{:S(2)}, u32[]{:S(2)}) %collective-permute-start) | collective-permute-done | bytes 655392 | tf_op jit(solution)/shard_map/ppermute | solution.py:158
  69.5 34.2 %collective-permute-done.2 = bf16[2,256,640]{2,1,0:T(8,128)(2,1)S(1)} collective-permute-done((bf16[2,256,640]{2,1,0:T(8,128)(2,1)}, bf16[2,256,640]{2,1,0:T(8,128)(2,1)S(1)}, u32[]{:S(2)}, u32[]{:S(2)}) %collective-permute-start.2) | collective-permute-done | bytes 655392 | tf_op jit(solution)/shard_map/ppermute | solution.py:158
  120.2 22.9 %collective-permute-done.4 = bf16[2,256,640]{2,1,0:T(8,128)(2,1)} collective-permute-done((bf16[2,256,640]{2,1,0:T(8,128)(2,1)S(1)}, bf16[2,256,640]{2,1,0:T(8,128)(2,1)}, u32[]{:S(2)}, u32[]{:S(2)}) %collective-permute-start.4) | collective-permute-done | bytes 655392 | tf_op jit(solution)/shard_map/ppermute | solution.py:158
  156.1 6.0 collective-permute-done.6
  164.4 7.3 slice_bitcast_fusion
  171.7 80.4 %while.43 = (s32[]{:T(128)}, bf16[10,768,64]{1,2,0:T(8,128)(2,1)S(1)}, f32[10,768]{1,0:T(8,128)S(1)}, f32[10,768]{1,0:T(8,128)S(1)}, bf16[10,768,64]{2,1,0:T(8,1...) while((s32[]{:T(128)}, ...), condition=%wide.region_4.5_spmd.clone, body=%wide.region_1.4_spmd.clone.sunk | while | flops 426244608 | bytes 19846260 | solution.py:175
  176.2 3.4 fusion.152
  184.2 3.3 fusion.152
  192.3 3.3 fusion.152
  200.3 3.3 fusion.152
  208.4 3.3 fusion.152
  216.4 3.3 fusion.152
  224.4 3.3 fusion.152
  232.5 3.3 fusion.152
  240.5 3.3 fusion.152
  248.6 3.3 fusion.152
  257.0 3.1 multiply_reduce_fusion.3
  262.4 7.5 fusion.58
  270.0 20.7 %all-gather.15.cloned.1.call-done = bf16[2,512,960]{1,2,0:T(8,128)(2,1)} async-done(((bf16[2,256,960]{1,2,0:T(8,128)(2,1)}), bf16[2,512,960]{1,2,0:T(8,128)(2,1)}) %all-gather.15.cloned.1.call-update) | async-done | bytes 1966096 | tf_op jit(solution)/shard_map/all_gather | solution.py:191
  290.7 7.6 fusion.64
  298.3 18.6 %all-gather.17.cloned.1.call-done = bf16[960,1280]{1,0:T(8,128)(2,1)} async-done(((bf16[240,1280]{1,0:T(8,128)(2,1)}), bf16[960,1280]{1,0:T(8,128)(2,1)}) %all-gather.17.cloned.1.call-update) | async-done | bytes 2457616 | tf_op jit(solution)/shard_map/all_gather | solution.py:182
  316.9 11.9 %multiply_convert_fusion.2 = (bf16[2,512,1280]{2,1,0:T(8,128)(2,1)S(1)}, bf16[2,512,1280]{2,1,0:T(8,128)(2,1)S(1)}, bf16[2,512,1280]{2,1,0:T(8,128)(2,1)}) fusion(f32[2,512,1280]{2,1,0:T(8,128)} %fusion.58, f32[2,512,1280]{2,1,0:T(8,128)} %fusion.64, bf16[2,512,960]{1,2,0:T(8,128)(2,1)} %all-gather.15.cloned.1.call-done, ...), kind=kOutput, calls=%fused_computation.71 | convolution fusion | flops 2536243200 | bytes 22773760 | tf_op jit(solution)/shard_map/dot_general | solution.py:194
  332.3 5.0 fusion.85
  337.4 6.5 fusion.88
  344.1 5.6 fusion.53
  349.7 3.4 bitcast_convert_fusion.2
  353.1 3.4 bitcast_convert_fusion.1
  356.6 3.4 pad_maximum_fusion.1
  359.9 29.6 %reduce-scatter.8.cloned.1.call-done = f32[2,256,960]{1,2,0:T(8,128)} async-done(((f32[2,512,960]{1,2,0:T(8,128)}), f32[2,256,960]{1,2,0:T(8,128)}) %reduce-scatter.8.cloned.1.call-update) | async-done | bytes 1966096 | tf_op jit(solution)/shard_map/reduce_scatter | solution.py:217
  392.3 29.9 %reduce-scatter.6.cloned.1.call-done = bf16[2,256,960]{1,2,0:T(8,128)(2,1)} async-done(((bf16[2,512,960]{1,2,0:T(8,128)(2,1)}), bf16[2,256,960]{1,2,0:T(8,128)(2,1)}) %reduce-scatter.6.cloned.1.call-update) | async-done | bytes 983056 | tf_op jit(solution)/shard_map/reduce_scatter | solution.py:200
  422.1 3.5 multiply_add_fusion
  428.7 340.2 %while.45 = (s32[]{:T(128)}, f32[2,5,768,64]{2,3,1,0:T(8,128)}, f32[2,256,640]{1,2,0:T(8,128)}, bf16[2,5,768,64]{3,2,1,0:T(8,128)(2,1)}, bf16[2,5,2048,64]{2,3,1...) while((s32[]{:T(128)}, f32[2,5,768,64]{2,3,1,0:T(8,128)}, ...), condition=%wide.region_14.15_spmd.clone, body=%wide.region_9.14_spmd.clone.sunk | while | flops 1025588480 | bytes 125203080 | solution.py:257
  436.8 3.1 copy.115
  442.9 79.9 %while.46 = (s32[]{:T(128)}, f32[5,768,64]{1,2,0:T(8,128)}, bf16[5,2048,64]{1,2,0:T(8,128)(2,1)}, bf16[5,2048,64]{1,2,0:T(8,128)(2,1)}, bf16[5,768,64]{2,1,0:T(8...) while((s32[]{:T(128)}, f32[5,768,64]{1,2,0:T(8,128)}, ...), condition=%wide.region_12.12_spmd, body=%wide.region_10.11_spmd.sunk | while | flops 1022541056 | bytes 79656208 | solution.py:231
  446.4 3.7 multiply_reduce_fusion.5
  462.4 3.7 multiply_reduce_fusion.5
  478.4 3.7 multiply_reduce_fusion.5
  494.3 3.7 multiply_reduce_fusion.5
  510.3 3.7 multiply_reduce_fusion.5
  522.8 3.5 pad_maximum_fusion.11
  528.5 68.9 %reduce-scatter.14.cloned.1.call-done = bf16[256,640]{0,1:T(8,128)(2,1)} async-done(((bf16[2048,640]{0,1:T(8,128)(2,1)}), bf16[256,640]{0,1:T(8,128)(2,1)}) %reduce-scatter.14.cloned.1.call-update) | async-done | bytes 327696 | tf_op jit(solution)/shard_map/while/body/eval_jaxpr/reduce_scatter | solution.py:239
  607.3 3.1 copy.115
  613.4 79.9 %while.46 = (s32[]{:T(128)}, f32[5,768,64]{1,2,0:T(8,128)}, bf16[5,2048,64]{1,2,0:T(8,128)(2,1)}, bf16[5,2048,64]{1,2,0:T(8,128)(2,1)}, bf16[5,768,64]{2,1,0:T(8...) while((s32[]{:T(128)}, f32[5,768,64]{1,2,0:T(8,128)}, ...), condition=%wide.region_12.12_spmd, body=%wide.region_10.11_spmd.sunk | while | flops 1022541056 | bytes 79656208 | solution.py:231
  617.0 3.7 multiply_reduce_fusion.5
  632.9 3.7 multiply_reduce_fusion.5
  648.9 3.7 multiply_reduce_fusion.5
  664.9 3.7 multiply_reduce_fusion.5
  680.8 3.7 multiply_reduce_fusion.5
  693.3 3.5 pad_maximum_fusion.11
  699.1 67.7 %reduce-scatter.14.cloned.1.call-done = bf16[256,640]{0,1:T(8,128)(2,1)} async-done(((bf16[2048,640]{0,1:T(8,128)(2,1)}), bf16[256,640]{0,1:T(8,128)(2,1)}) %reduce-scatter.14.cloned.1.call-update) | async-done | bytes 327696 | tf_op jit(solution)/shard_map/while/body/eval_jaxpr/reduce_scatter | solution.py:239
  771.3 3.1 reshape_reshape.14
  787.2 9.3 concatenate.38
  796.6 40.3 %reduce-scatter.12.cloned.1.call-done = bf16[240,3840]{1,0:T(8,128)(2,1)} async-done(((bf16[960,3840]{1,0:T(8,128)(2,1)}), bf16[240,3840]{1,0:T(8,128)(2,1)}) %reduce-scatter.12.cloned.1.call-update) | async-done | bytes 1843216 | tf_op jit(solution)/shard_map/reduce_scatter | solution.py:302
  837.7 3.1 fusion.81
  843.4 5.7 all-reduce.5
  849.2 21.5 %all-reduce.4 = (bf16[240]{0:T(256)(128)(2,1)S(1)}, bf16[240]{0:T(256)(128)(2,1)S(1)}) all-reduce(bf16[240]{0:T(256)(128)(2,1)S(1)} %dynamic-slice.3, bf16[240]{0:T(256)(128)(2,1)S(1)} %dynamic-slice.5), channel_id=1, replica_groups=mesh['fsdp'=4,'ctx'=4,'tp'=2] {'ctx','tp'}, use_global_device_ids=true, to_apply=%region_17.18 | all-reduce | flops 480 | bytes 1920 | tf_op jit(solution)/shard_map/psum | solution.py:294
  871.9 16.8 %reduce-scatter.10.cloned.1.call-done = bf16[240,2560]{1,0:T(8,128)(2,1)} async-done(((bf16[960,2560]{1,0:T(8,128)(2,1)}), bf16[240,2560]{1,0:T(8,128)(2,1)}) %reduce-scatter.10.cloned.1.call-update) | async-done | bytes 1228816 | tf_op jit(solution)/shard_map/reduce_scatter | solution.py:299
  888.8 3.3 fusion.74
  892.1 77.4 %all-reduce.12.cloned.1.call-done = bf16[240,3840]{1,0:T(8,128)(2,1)} async-done(((bf16[240,3840]{1,0:T(8,128)(2,1)}), bf16[240,3840]{1,0:T(8,128)(2,1)}) %all-reduce.12.cloned.1.call-update) | async-done | bytes 1843216 | tf_op jit(solution)/shard_map/psum | solution.py:297
  969.5 3.4 fusion.112
  972.8 80.3 %all-reduce.10.cloned.1.call-done = bf16[240,2560]{1,0:T(8,128)(2,1)} async-done(((bf16[240,2560]{1,0:T(8,128)(2,1)}), bf16[240,2560]{1,0:T(8,128)(2,1)}) %all-reduce.10.cloned.1.call-update) | async-done | bytes 1228816 | tf_op jit(solution)/shard_map/psum | solution.py:293
  (454 shorter events, 286.3 us)
Async XLA Ops:
  7.2 3.5 copy-start.35
  7.2 4.7 copy-start.41
  7.2 5.0 copy-start.42
  7.2 13.6 %copy-start.11 = (bf16[2,256,960]{1,2,0:T(8,128)(2,1)S(1)}, bf16[2,256,960]{1,2,0:T(8,128)(2,1)}, u32[]{:S(2)}) copy-start(bf16[2,256,960]{1,2,0:T(8,128)(2,1)} %param.16) | copy-start | bytes 2949124
  7.2 22.9 %all-gather.11.cloned.1.call-start = ((), (), s32[]{:S(2)}) async-start(), calls=%async_computation.6 | async-start | bytes 1536000 | tf_op jit(solution)/shard_map/all_gather | solution.py:125
  8.0 106.6 %all-gather.9.cloned.1.call-start = ((), (), s32[]{:S(2)}) async-start(), calls=%async_computation.5 | async-start | bytes 2457600 | tf_op jit(solution)/shard_map/all_gather | solution.py:124
  8.7 248.3 %all-gather.13.cloned.1.call-start = ((), (), s32[]{:S(2)}) async-start(), calls=%async_computation.7 | async-start | bytes 2457600 | tf_op jit(solution)/shard_map/all_gather | solution.py:126
  9.4 253.0 %all-gather.23.cloned.1.call-start = ((), (), s32[]{:S(2)}) async-start(), calls=%async_computation.13 | async-start | bytes 2949120 | tf_op jit(solution)/shard_map/all_gather | solution.py:192
  10.0 252.4 %all-gather.21.cloned.1.call-start = ((), (), s32[]{:S(2)}) async-start(), calls=%async_computation.11 | async-start | bytes 3072000 | tf_op jit(solution)/shard_map/all_gather | solution.py:184
  10.6 259.4 %all-gather.19.cloned.1.call-start = ((), (), s32[]{:S(2)}) async-start(), calls=%async_computation.10 | async-start | bytes 3072000 | tf_op jit(solution)/shard_map/all_gather | solution.py:183
  20.8 93.8 %copy-start.30 = (f32[960]{0:T(1024)}, f32[960]{0:T(1024)S(1)}, u32[]{:S(2)}) copy-start(f32[960]{0:T(1024)S(1)} %convert_element_type.123) | copy-start | bytes 11524
  21.0 93.5 %copy-start.33 = (f32[2,256]{1,0:T(2,128)}, f32[2,256]{1,0:T(2,128)S(1)}, u32[]{:S(2)}) copy-start(f32[2,256]{1,0:T(2,128)S(1)} %add_rsqrt_fusion.1) | copy-start | bytes 6148
  21.9 124.0 %copy-start.21 = (f32[256,32]{0,1:T(8,128)}, f32[256,32]{0,1:T(8,128)S(1)}, u32[]{:S(2)}) copy-start(f32[256,32]{0,1:T(8,128)S(1)} %get-tuple-element.374) | copy-start | bytes 98308
  33.6 30.0 %collective-permute-start = (bf16[2,256,640]{2,1,0:T(8,128)(2,1)S(1)}, bf16[2,256,640]{2,1,0:T(8,128)(2,1)}, u32[]{:S(2)}, u32[]{:S(2)}) collective-permute-start(bf16[2,256,640]{2,1,0:T(8,128)(2,1)S(1)} %pad_maximum_fusion.4), channel_id=1, source_target_pairs={{0,1},{1,2},{2,3},{3,4},{4,5},{5,6},{6,7},{7,0},{8,9},{9,10},{10,1... | collective-permute-start | bytes 1966088 | tf_op jit(solution)/shard_map/ppermute | solution.py:158
  35.1 31.6 %collective-permute-start.1 = (bf16[2,256,640]{2,1,0:T(8,128)(2,1)S(1)}, bf16[2,256,640]{2,1,0:T(8,128)(2,1)}, u32[]{:S(2)}, u32[]{:S(2)}) collective-permute-start(bf16[2,256,640]{2,1,0:T(8,128)(2,1)S(1)} %pad_maximum_fusion.4), channel_id=1, source_target_pairs={{0,7},{1,0},{2,1},{3,2},{4,3},{5,4},{6,5},{7,6},{8,15},{9,8},{10,9... | collective-permute-start | bytes 1966088 | tf_op jit(solution)/shard_map/ppermute | solution.py:163
  63.6 40.1 %collective-permute-start.2 = (bf16[2,256,640]{2,1,0:T(8,128)(2,1)}, bf16[2,256,640]{2,1,0:T(8,128)(2,1)S(1)}, u32[]{:S(2)}, u32[]{:S(2)}) collective-permute-start(bf16[2,256,640]{2,1,0:T(8,128)(2,1)} %collective-permute-done), channel_id=1, source_target_pairs={{0,1},{1,2},{2,3},{3,4},{4,5},{5,6},{6,7},{7,0},{8,9},{9,10},{10,1... | collective-permute-start | bytes 1966088 | tf_op jit(solution)/shard_map/ppermute | solution.py:158
  66.2 224.5 %all-gather.15.cloned.1.call-start = ((), (), s32[]{:S(2)}) async-start(), calls=%async_computation.8 | async-start | bytes 2949120 | tf_op jit(solution)/shard_map/all_gather | solution.py:191
  66.7 53.5 %collective-permute-start.3 = (bf16[2,256,640]{2,1,0:T(8,128)(2,1)}, bf16[2,256,640]{2,1,0:T(8,128)(2,1)}, u32[]{:S(2)}, u32[]{:S(2)}) collective-permute-start(bf16[2,256,640]{2,1,0:T(8,128)(2,1)} %collective-permute-done.1), channel_id=1, source_target_pairs={{0,7},{1,0},{2,1},{3,2},{4,3},{5,4},{6,5},{7,6},{8,15},{9,8},{10,9... | collective-permute-start | bytes 1966088 | tf_op jit(solution)/shard_map/ppermute | solution.py:163
  103.7 5.4 copy-start.23
  103.7 39.5 %collective-permute-start.4 = (bf16[2,256,640]{2,1,0:T(8,128)(2,1)S(1)}, bf16[2,256,640]{2,1,0:T(8,128)(2,1)}, u32[]{:S(2)}, u32[]{:S(2)}) collective-permute-start(bf16[2,256,640]{2,1,0:T(8,128)(2,1)S(1)} %collective-permute-done.2), channel_id=1, source_target_pairs={{0,1},{1,2},{2,3},{3,4},{4,5},{5,6},{6,7},{7,0},{8,9},{9,10},{10,1... | collective-permute-start | bytes 1966088 | tf_op jit(solution)/shard_map/ppermute | solution.py:158
  120.2 32.7 %collective-permute-start.5 = (bf16[2,256,640]{2,1,0:T(8,128)(2,1)}, bf16[2,256,640]{2,1,0:T(8,128)(2,1)}, u32[]{:S(2)}, u32[]{:S(2)}) collective-permute-start(bf16[2,256,640]{2,1,0:T(8,128)(2,1)} %collective-permute-done.3), channel_id=1, source_target_pairs={{0,7},{1,0},{2,1},{3,2},{4,3},{5,4},{6,5},{7,6},{8,15},{9,8},{10,9... | collective-permute-start | bytes 1966088 | tf_op jit(solution)/shard_map/ppermute | solution.py:163
  143.1 19.0 %collective-permute-start.6 = (bf16[2,256,640]{2,1,0:T(8,128)(2,1)}, bf16[2,256,640]{2,1,0:T(8,128)(2,1)}, u32[]{:S(2)}, u32[]{:S(2)}) collective-permute-start(bf16[2,256,640]{2,1,0:T(8,128)(2,1)} %collective-permute-done.4), channel_id=1, source_target_pairs={{0,1},{1,2},{2,3},{3,4},{4,5},{5,6},{6,7},{7,0},{8,9},{9,10},{10,1... | collective-permute-start | bytes 1966088 | tf_op jit(solution)/shard_map/ppermute | solution.py:158
  146.3 3.1 copy-start.24
  164.4 7.3 copy-start.18
  261.4 55.5 %all-gather.17.cloned.1.call-start = ((), (), s32[]{:S(2)}) async-start(), calls=%async_computation.9 | async-start | bytes 3072000 | tf_op jit(solution)/shard_map/all_gather | solution.py:182
  262.1 127.4 %reduce-scatter.8.cloned.1.call-start = ((), (), s32[]{:S(2)}) async-start(), calls=%async_computation.14 | async-start | bytes 5898240 | tf_op jit(solution)/shard_map/reduce_scatter | solution.py:217
  316.9 11.9 %copy-start.36 = (bf16[960,1280]{1,0:T(8,128)(2,1)S(1)}, bf16[960,1280]{1,0:T(8,128)(2,1)}, u32[]{:S(2)}) copy-start(bf16[960,1280]{1,0:T(8,128)(2,1)} %all-gather.19.cloned.1.call-done) | copy-start | bytes 7372804
  328.8 3.5 copy-start.37
  337.4 84.7 %reduce-scatter.6.cloned.1.call-start = ((), (), s32[]{:S(2)}) async-start(), calls=%async_computation.12 | async-start | bytes 2949120 | tf_op jit(solution)/shard_map/reduce_scatter | solution.py:200
  344.1 5.6 copy-start.39
  344.1 5.6 copy-start.46
  349.7 3.5 copy-start.44
  359.9 62.2 %copy-start.10 = (bf16[2,256,960]{1,2,0:T(8,128)(2,1)S(1)}, bf16[2,256,960]{1,2,0:T(8,128)(2,1)}, u32[]{:S(2)}) copy-start(bf16[2,256,960]{1,2,0:T(8,128)(2,1)} %param.17) | copy-start | bytes 2949124
  422.1 3.5 copy-start.38
  428.9 168.5 %reduce-scatter.14.cloned.1.call-start = ((), (), s32[]{:S(2)}) async-start(), calls=%async_computation.19 | async-start | bytes 2949120 | tf_op jit(solution)/shard_map/while/body/eval_jaxpr/reduce_scatter | solution.py:239
  453.1 2.9 copy-start.3
  456.0 2.9 copy-start.1
  469.1 2.9 copy-start.3
  472.0 2.9 copy-start.1
  485.0 2.9 copy-start.3
  488.0 2.9 copy-start.1
  501.0 2.9 copy-start.3
  503.9 2.9 copy-start.1
  517.0 2.9 copy-start.3
  519.9 2.9 copy-start.1
  526.3 71.1 %copy-start.13 = (f32[2,256,640]{1,2,0:T(8,128)S(1)}, f32[2,256,640]{1,2,0:T(8,128)}, u32[]{:S(2)}) copy-start(f32[2,256,640]{1,2,0:T(8,128)} %get-tuple-element.691) | copy-start | bytes 3932164 | tf_op jit(solution)/shard_map/while
  599.5 167.3 %reduce-scatter.14.cloned.1.call-start = ((), (), s32[]{:S(2)}) async-start(), calls=%async_computation.19 | async-start | bytes 2949120 | tf_op jit(solution)/shard_map/while/body/eval_jaxpr/reduce_scatter | solution.py:239
  623.6 2.9 copy-start.3
  626.5 2.9 copy-start.1
  639.6 2.9 copy-start.3
  642.5 2.9 copy-start.1
  655.6 2.9 copy-start.3
  658.5 2.9 copy-start.1
  671.5 2.9 copy-start.3
  674.4 2.9 copy-start.1
  687.5 2.9 copy-start.3
  696.8 70.0 %copy-start.13 = (f32[2,256,640]{1,2,0:T(8,128)S(1)}, f32[2,256,640]{1,2,0:T(8,128)}, u32[]{:S(2)}) copy-start(f32[2,256,640]{1,2,0:T(8,128)} %get-tuple-element.691) | copy-start | bytes 3932164 | tf_op jit(solution)/shard_map/while
  768.9 68.0 %reduce-scatter.12.cloned.1.call-start = ((), (), s32[]{:S(2)}) async-start(), calls=%async_computation.17 | async-start | bytes 9216000 | tf_op jit(solution)/shard_map/reduce_scatter | solution.py:302
  769.6 119.2 %reduce-scatter.10.cloned.1.call-start = ((), (), s32[]{:S(2)}) async-start(), calls=%async_computation.15 | async-start | bytes 6144000 | tf_op jit(solution)/shard_map/reduce_scatter | solution.py:299
  796.5 172.9 %all-reduce.12.cloned.1.call-start = ((), (), s32[]{:S(2)}) async-start(), calls=%async_computation.18 | async-start | bytes 3686400 | tf_op jit(solution)/shard_map/psum | solution.py:297
  836.9 216.1 %all-reduce.10.cloned.1.call-start = ((), (), s32[]{:S(2)}) async-start(), calls=%async_computation.16 | async-start | bytes 2457600 | tf_op jit(solution)/shard_map/psum | solution.py:293
  837.6 3.1 copy-start.26
  837.6 3.1 copy-start.28
  837.7 3.1 copy-start.40
  (54 other events, 91.1 us)
Sparse Core Ops, SparseCore 0:
  9.6 20.4 all-gather.10
  31.6 21.8 all-gather.8
  55.1 21.8 all-gather.12
  78.4 65.1 all-gather.22
  145.0 23.8 all-gather.20
  170.3 24.6 all-gather.18
  261.5 29.1 all-gather.14
  292.2 24.6 all-gather.16
  337.5 51.9 reduce-scatter.7
  391.7 30.3 reduce-scatter.5
  526.4 70.9 reduce-scatter.13
  697.0 69.7 reduce-scatter.13
  772.2 64.6 reduce-scatter.11
  839.5 49.1 reduce-scatter.9
  891.0 78.4 all-reduce.11
  972.9 80.1 all-reduce.9
